TPU v7x, 512 devices: a whole 4x4x16 slice. The times are simulated.
512 devices in a mesh: row: 16 (over y, x), col: 32 (over z, core).
Axes of the slice: x: 4, y: 4, z: 16, core: 2. Of those that a mesh axis runs over, the one named last changes fastest.
Arguments:
- features: bfloat16 [65536, 128], P(('col', 'row')), may hold values from -6 to 6
- tiles: bfloat16 [16, 32, 16, 128, 128], P('row', 'col'), may hold values from -0.25 to 0.25
- tile_rows: int32 [16, 32, 16], P('row', 'col'), may hold values from 0 to 31, as said below
- tile_cols: int32 [16, 32, 16], P('row', 'col'), may hold values from 0 to 15, as said below
- tile_count: int32 [16, 32], P('row', 'col'), may hold values from 2 to 16, as said below
- weight: float32 [128, 256], replicated, may hold values from -0.5 to 0.5
- bias: float32 [256], replicated, may hold values from -3 to 3
- cotangent: bfloat16 [65536, 256], P(('row', 'col')), may hold values from -6 to 6
Outputs:
- output: bfloat16 [65536, 256], P(('row', 'col'))
- grad_features: bfloat16 [65536, 128], P(('col', 'row'))
- grad_weight: float32 [128, 256], replicated
- grad_bias: float32 [256], replicated
Inputs may be any that keep to these rules, and one draw needn't show every extreme that they name: `tile_rows`: within one device the live slots name distinct tile places; dead slots hold values that are not part of A. `tile_cols`: distinct places within one device, together with tile_rows. `tile_count`: some device has all 16 slots live.
All inputs are finite; a program needn't handle non-finite values.
Results may differ from a plain program's by a relative error of at most 0.023.
Values may be sent and summed in bfloat16 or wider, within the bound.
A program may use at most 128 MiB of HBM per device.

v0:
```python
import jax
import jax.numpy as jnp
from jax import lax
from jax.sharding import PartitionSpec as P

BR = 32


def on_device(features, tiles, tile_rows, tile_cols, tile_count, weight, bias, cotangent):
    high = lax.Precision.HIGHEST
    blocks = tiles.reshape(tiles.shape[2], tiles.shape[3], tiles.shape[4])
    size = blocks.shape[1]
    width = features.shape[1]
    rows = tile_rows.reshape(-1)
    cols = tile_cols.reshape(-1)
    live = (jnp.arange(blocks.shape[0]) < tile_count.reshape(())).astype(jnp.float32)
    column_feats = lax.all_gather(features, "row", axis=0, tiled=True)
    ncolblocks = column_feats.shape[0] // size
    picked = column_feats.reshape(ncolblocks, size, width)[cols]
    products = jnp.einsum("kij,kjf->kif", blocks, picked, preferred_element_type=jnp.float32)
    row_onehot = (rows[:, None] == jnp.arange(BR)[None, :]).astype(jnp.float32) * live[:, None]
    partial_value = jnp.einsum("kb,kif->bif", row_onehot, products, precision=high).reshape(
        BR * size, width
    )
    aggregated = lax.psum_scatter(
        partial_value.astype(jnp.bfloat16), "col", scatter_dimension=0, tiled=True
    )
    agg_float = aggregated.astype(jnp.float32)
    pre = jnp.dot(agg_float, weight, precision=high) + bias
    value, act_vjp = jax.vjp(jax.nn.gelu, pre)
    output = value.astype(jnp.bfloat16)
    dpre = act_vjp(cotangent.astype(jnp.float32))[0]
    local_weight = jnp.dot(agg_float.T, dpre, precision=high)
    local_bias = jnp.sum(dpre, axis=0)
    grad_weight, grad_bias = lax.psum((local_weight, local_bias), ("row", "col"))
    daggregated = jnp.dot(dpre, weight.T, precision=high).astype(jnp.bfloat16)
    block_grads = lax.all_gather(daggregated, "col", axis=0, tiled=True)
    picked_grads = block_grads.reshape(BR, size, width)[rows]
    back = jnp.einsum("kji,kjf->kif", blocks, picked_grads, preferred_element_type=jnp.float32)
    col_onehot = (cols[:, None] == jnp.arange(ncolblocks)[None, :]).astype(jnp.float32) * live[
        :, None
    ]
    back_partial = jnp.einsum("kb,kif->bif", col_onehot, back, precision=high).reshape(
        ncolblocks * size, width
    )
    grad_features = lax.psum_scatter(
        back_partial.astype(jnp.bfloat16), "row", scatter_dimension=0, tiled=True
    )
    return (output, grad_features, grad_weight, grad_bias)


def solution(mesh):
    placed = (
        P(("col", "row"), None),
        P("row", "col", None, None, None),
        P("row", "col", None),
        P("row", "col", None),
        P("row", "col"),
        P(),
        P(),
        P(("row", "col"), None),
    )
    return jax.shard_map(
        on_device,
        mesh=mesh,
        in_specs=placed,
        out_specs=(P(("row", "col"), None), P(("col", "row"), None), P(), P()),
        check_vma=False,
    )
```

profile of v0, /device:TPU:1, one launch (start us, length us, event | category | flops | bytes accessed | tf_op | source)
XLA Modules:
  0.0 762.2 jit_solution(11004990129254970327)
XLA Ops:
  7.2 0.0 copy-start
  7.2 0.0 reduce-scatter.3.cloned.1.call-start
  7.9 0.7 fusion.25
  8.6 20.0 %all_gather.6 = bf16[2048,128]{1,0:T(8,128)(2,1)S(1)} all-gather(bf16[128,128]{1,0:T(8,128)(2,1)} %param.8), channel_id=1, replica_groups=mesh['row'=16,'col'=32] {'row'}, dimensions={0}, use_global_device_ids=true | all-gather | bytes 557056 | tf_op jit(solution)/shard_map/all_gather | solution.py:17
  28.6 0.6 gather_fusion
  29.2 0.0 copy-done
  29.2 0.5 fusion.4
  29.8 0.0 copy-start.4
  29.8 0.5 copy.14
  30.3 0.1 copy-done.4
  30.4 1.9 convolution_convert_fusion
  32.3 1.4 copy.12
  33.7 0.0 copy-start.1
  33.7 0.0 copy-start.5
  33.7 0.0 copy-start.6
  33.7 0.0 reduce-scatter.3.cloned.1.call-update
  33.7 0.0 all-gather.2.cloned.1.call-start
  33.8 112.9 %reduce-scatter.3.cloned.1.call-done = bf16[128,128]{1,0:T(8,128)(2,1)} async-done(((bf16[4096,128]{1,0:T(8,128)(2,1)}), bf16[128,128]{1,0:T(8,128)(2,1)}) %reduce-scatter.3.cloned.1.call-update) | async-done | bytes 32784 | tf_op jit(solution)/shard_map/reduce_scatter | solution.py:25
  146.7 0.0 copy-done.1
  146.7 0.0 copy-done.5
  146.7 0.0 copy-done.6
  146.7 0.0 copy-start.2
  146.7 1.8 fusion.29
  148.4 0.9 convolution_convert_fusion.2
  149.3 0.0 all-gather.2.cloned.1.call-update
  149.4 0.0 all-reduce.2.cloned.1.call-start
  149.4 0.0 copy-done.2
  149.5 0.9 fusion.31
  150.4 0.0 all-reduce.2.cloned.1.call-update
  150.4 0.0 reduce-scatter.5.cloned.1.call-start
  150.5 70.9 %all-gather.2.cloned.1.call-done = bf16[4096,128]{1,0:T(8,128)(2,1)} async-done(((bf16[128,128]{1,0:T(8,128)(2,1)}), bf16[4096,128]{1,0:T(8,128)(2,1)}) %all-gather.2.cloned.1.call-update) | async-done | bytes 1048592 | tf_op jit(solution)/shard_map/all_gather | solution.py:37
  221.3 1.9 gather_fusion.1
  223.2 0.4 fusion.2
  223.6 0.0 copy-start.3
  223.6 0.5 copy.15
  224.1 0.1 copy-done.3
  224.2 1.0 convolution_convert_fusion.1
  225.2 0.9 copy.13
  226.2 0.0 reduce-scatter.5.cloned.1.call-update
  226.2 103.1 %psum.15 = f32[256]{0:T(256)} all-reduce(f32[256]{0:T(256)S(1)} %get-tuple-element.4), channel_id=1, replica_groups=mesh['row'=16,'col'=32] {'row','col'}, use_global_device_ids=true, to_apply=%region_4.0 | all-reduce | flops 256 | bytes 2048 | tf_op jit(solution)/shard_map/psum | solution.py:35
  329.3 344.3 %all-reduce.2.cloned.1.call-done = f32[128,256]{1,0:T(8,128)} async-done(((f32[128,256]{1,0:T(8,128)}), f32[128,256]{1,0:T(8,128)}) %all-reduce.2.cloned.1.call-update) | async-done | bytes 131088 | tf_op jit(solution)/shard_map/psum | solution.py:35
  673.6 80.5 %reduce-scatter.5.cloned.1.call-done = bf16[128,128]{1,0:T(8,128)(2,1)} async-done(((bf16[2048,128]{1,0:T(8,128)(2,1)}), bf16[128,128]{1,0:T(8,128)(2,1)}) %reduce-scatter.5.cloned.1.call-update) | async-done | bytes 32784 | tf_op jit(solution)/shard_map/reduce_scatter | solution.py:46
  754.1 1.6 copy.18
  (4 shorter events, 0.0 us)
Async XLA Ops:
  7.2 22.1 %copy-start = (bf16[1,1,16,128,128]{4,3,2,1,0:T(8,128)(2,1)S(1)}, bf16[1,1,16,128,128]{4,3,2,1,0:T(8,128)(2,1)}, u32[]{:S(2)}) copy-start(bf16[1,1,16,128,128]{4,3,2,1,0:T(8,128)(2,1)} %param.9) | copy-start | bytes 1572868
  7.2 139.5 %reduce-scatter.3.cloned.1.call-start = ((), (), s32[]{:S(2)}) async-start(), calls=%async_computation.2 | async-start | bytes 1081344 | tf_op jit(solution)/shard_map/reduce_scatter | solution.py:25
  29.8 0.7 copy-start.4
  33.7 113.0 %copy-start.1 = (f32[128,256]{1,0:T(8,128)S(1)}, f32[128,256]{1,0:T(8,128)}, u32[]{:S(2)}) copy-start(f32[128,256]{1,0:T(8,128)} %param.13) | copy-start | bytes 393220
  33.7 113.0 %copy-start.5 = (bf16[128,256]{1,0:T(8,128)(2,1)S(1)}, bf16[128,256]{1,0:T(8,128)(2,1)}, u32[]{:S(2)}) copy-start(bf16[128,256]{1,0:T(8,128)(2,1)} %param.15) | copy-start | bytes 196612
  33.7 113.0 %copy-start.6 = (f32[256]{0:T(256)S(1)}, f32[256]{0:T(256)}, u32[]{:S(2)}) copy-start(f32[256]{0:T(256)} %param.14) | copy-start | bytes 3076
  33.7 187.6 %all-gather.2.cloned.1.call-start = ((), (), s32[]{:S(2)}) async-start(), calls=%async_computation.3 | async-start | bytes 1081344 | tf_op jit(solution)/shard_map/all_gather | solution.py:37
  146.7 2.8 copy-start.2
  149.4 524.2 %all-reduce.2.cloned.1.call-start = ((), (), s32[]{:S(2)}) async-start(), calls=%async_computation.5 | async-start | bytes 262144 | tf_op jit(solution)/shard_map/psum | solution.py:35
  150.4 603.7 %reduce-scatter.5.cloned.1.call-start = ((), (), s32[]{:S(2)}) async-start(), calls=%async_computation.4 | async-start | bytes 557056 | tf_op jit(solution)/shard_map/reduce_scatter | solution.py:46
  223.6 0.7 copy-start.3
Sparse Core Ops, SparseCore 0:
  33.9 112.7 reduce-scatter.2
  149.6 71.7 all-gather.1
  228.2 445.2 all-reduce.1
  678.1 75.9 reduce-scatter.4
where the time goes:
time: 763 us; the launch traced here: 762 us
  waiting for transfers between devices  609 us (80%)
  blocking collectives  123 us (16%)
  between operations  14.6 us (2%)
  local copies, waits for them, and re-layouts  7.71 us (1%)
    psum x1, waiting for transfers between devices, on_device(): lax.psum((local_weight, local_bias), ('row', 'col'))  344 us
    reduce_scatter x1, waiting for transfers between devices, on_device(): lax.psum_scatter(partial_value.astype(jnp.bfloat16), 'col', scatter_dimen...  113 us
    psum x1, blocking collectives, on_device(): lax.psum((local_weight, local_bias), ('row', 'col'))  103 us
    reduce_scatter x1, waiting for transfers between devices, on_device(): lax.psum_scatter(back_partial.astype(jnp.bfloat16), 'row', scatter_dimens...  80.5 us
    all_gather x1, waiting for transfers between devices, on_device(): block_grads = lax.all_gather(daggregated, 'col', axis=0, tiled=True)  70.9 us
    all_gather x1, blocking collectives, on_device(): column_feats = lax.all_gather(features, 'row', axis=0, tiled=True)  20 us
  transfers between devices with their start and end apart: 4, of which 4 were waited for; matrix products, arithmetic and copies ran while one was open for 1% of the time, Pallas kernels for 0%

commit v1 on v0

v1 whole, which is shorter than its diff:
```python
import jax
import jax.numpy as jnp
from jax import lax
from jax.experimental import pallas as pl
from jax.experimental.pallas import tpu as pltpu
from jax.sharding import PartitionSpec as P

MESH = pl.DeviceIdType.MESH
F32 = jnp.float32
BF16 = jnp.bfloat16
T = 128
K = 16
NX = 4
NY = 4
NZ = 16
NP = NX * NY
BR = 32
NODES = 65536
HID = 256
LEAF = {5: 6, 7: 6, 8: 6, -4: -5, -6: -5, -7: -5, 2: 3, 4: 3, -3: -2}
RELAY = [6, -5, 3, -2]
NEAR = [1, -1]
ORDER = list(LEAF) + NEAR + RELAY + [0]
AT = {p: n for n, p in enumerate(ORDER)}
C0 = 0.7978845608028654
C1 = 0.044715


def dot(a, b, dims=((1,), (0,))):
    return lax.dot_general(a, b, (dims, ((), ())), preferred_element_type=F32)


def split(v):
    hi = v.astype(BF16)
    return hi, (v - hi.astype(F32)).astype(BF16)


def kernel(
    feat, tiles_hbm, rows, cols, count, w_hbm, bias, cot_hbm,
    out, gf, gw, gb,
    tiles, w, cot, feats, sums, part, sib, bsend, brecv, dagg, qpart, qrecv,
    epart, erecv, ehalf, esib, zmine, zrecv, fin, gwrecv,
    in_sem, a_ss, a_rs, p_ss, p_rs, b_ss, b_rs,
    c_ss, c_rs, cs_ss, cs_rs, q_ss, q_rs,
    e_ss, e_rs, es_ss, es_rs, z_ss, z_rs, g_ss, g_rs,
):
    r = lax.axis_index("row")
    c = lax.axis_index("col")
    y, x = r // NX, r % NX
    z, core = c // 2, c % 2

    def plane(i):
        return ((y + i // NX) % NY) * NX + (x + i % NX) % NX

    def ring(i):
        return ((z + i) % NZ) * 2 + core

    me_other = (r, z * 2 + 1 - core)
    loads = [
        pltpu.make_async_copy(a, b, in_sem.at[n])
        for n, (a, b) in enumerate(
            ((feat, feats.at[r]), (tiles_hbm, tiles), (w_hbm, w), (cot_hbm, cot))
        )
    ]
    for copy in loads:
        copy.start()
    started = []

    def send(src, dst, ssem, rsem, where):
        copy = pltpu.make_async_remote_copy(
            src_ref=src, dst_ref=dst, send_sem=ssem, recv_sem=rsem,
            device_id=where, device_id_type=MESH,
        )
        copy.start()
        started.append(copy)
        return copy

    barrier = pltpu.get_barrier_semaphore()
    for i in range(1, NP):
        pl.semaphore_signal(barrier, inc=1, device_id=(plane(i), c), device_id_type=MESH)
    for i in range(1, NZ):
        pl.semaphore_signal(barrier, inc=1, device_id=(r, ring(i)), device_id_type=MESH)
    pl.semaphore_signal(barrier, inc=1, device_id=me_other, device_id_type=MESH)
    pl.semaphore_wait(barrier, NP + NZ - 1)

    a_copies = [
        send(feat, feats.at[r], a_ss.at[i], a_rs.at[i], (plane(i), c))
        for i in range(1, NP)
    ]

    live = count[0]
    dead = [NODES * jnp.minimum(jnp.maximum(k + 1 - live, 0), 1) for k in range(K)]
    slot_r = [rows[k] + dead[k] for k in range(K)]
    slot_c = [cols[k] + dead[k] for k in range(K)]

    def latest(slots, n, b):
        found = jnp.int32(0)
        for k in range(n):
            apart = slots[k] - b
            differs = jnp.minimum(jnp.maximum(apart, -apart), 1)
            found = jnp.maximum(found, (k + 1) * (1 - differs))
        return found

    prev_r = [latest(slot_r, k, slot_r[k]) for k in range(K)]
    prev_c = [latest(slot_c, k, slot_c[k]) for k in range(K)]
    last_r = [
        [latest(slot_r, K, ring(NZ - p) // 2 * 2 + half) for p in ORDER]
        for half in (1 - core, core)
    ]
    last_c = [latest(slot_c, K, plane(i)) for i in range(NP)]

    sums[0] = jnp.zeros((T, T), F32)
    for copy in loads:
        copy.wait()
    for copy in a_copies:
        copy.wait_recv()

    for k in range(K):
        sums[k + 1] = dot(tiles[k], feats[jnp.minimum(jnp.maximum(cols[k], 0), NP - 1)])
    for k in range(1, K):
        sums[k + 1] = sums[k + 1] + sums[prev_r[k]]

    p_copies = []
    for g in range(4):
        for j in range(4 * g, 4 * g + 4):
            part[0, j] = sums[last_r[0][j]].astype(BF16)
        four = pl.ds(4 * g, 4)
        p_copies.append(
            send(part.at[0, four], sib.at[four], p_ss.at[g], p_rs.at[g], me_other)
        )
    for j in range(NZ):
        part[1, j] = sums[last_r[1][j]].astype(BF16)

    b_copies = {}

    def own(p):
        j = AT[p]
        if j % 4 == 0:
            p_copies[j // 4].wait_recv()
        return part[1, j].astype(F32) + sib[j].astype(F32)

    def pass_on(p, to):
        v = own(p)
        for leaf, relay in LEAF.items():
            if relay == p:
                b_copies[leaf].wait_recv()
                v = v + brecv[AT[leaf]].astype(F32)
        n = AT[p]
        bsend[n] = v.astype(BF16)
        b_copies[p] = send(
            bsend.at[n], brecv.at[n], b_ss.at[n], b_rs.at[n], (r, ring(NZ + to - p))
        )

    for p in ORDER[:-1]:
        pass_on(p, LEAF.get(p, 0))
    total = own(0)
    for p in NEAR + RELAY:
        b_copies[p].wait_recv()
        total = total + brecv[AT[p]].astype(F32)
    agg = total.astype(BF16)

    w_hi, w_lo = split(w[...])
    pre = dot(agg, w_hi) + dot(agg, w_lo) + bias[...]
    square = pre * pre
    t = jnp.tanh(C0 * (pre + C1 * (square * pre)))
    half = 0.5 * (1.0 + t)
    slope = half + 0.5 * pre * (1.0 - t * t) * (C0 * (1.0 + 3.0 * C1 * square))
    dpre = cot[...].astype(F32) * slope
    dp_hi, dp_lo = split(dpre)
    back = ((1,), (1,))
    da = dot(dp_hi, w_hi, back) + dot(dp_lo, w_hi, back) + dot(dp_hi, w_lo, back)
    dagg[c] = da.astype(BF16)

    c_copies = {}

    def c_send(p, via):
        block = dagg.at[ring(NZ - via)]
        n = AT[p]
        c_copies[p] = send(
            block, block, c_ss.at[n], c_rs.at[n], (r, ring(NZ + p - via))
        )

    cs_copies = []

    def c_share(p):
        block = dagg.at[ring(NZ - p)]
        n = AT[p]
        cs_copies.append(send(block, block, cs_ss.at[n], cs_rs.at[n], me_other))

    for p in RELAY + NEAR:
        c_send(p, 0)
    c_share(0)

    out[...] = (pre * half).astype(BF16)
    down0 = ((0,), (0,))
    local_w = dot(agg, dp_hi, down0) + dot(agg, dp_lo, down0)
    local_b = jnp.sum(dpre.reshape(T // 8, 8, HID), axis=0)
    for p in range(NP):
        epart[p, 0:8] = local_w[8 * p : 8 * p + 8]
        epart[p, 8:16] = local_b
    e_copies = [
        send(epart.at[plane(i)], erecv.at[i], e_ss.at[i], e_rs.at[i], (plane(i), c))
        for i in range(1, NP)
    ]

    for via in RELAY:
        c_copies[via].wait_recv()
        for p, relay in LEAF.items():
            if relay == via:
                c_send(p, via)
        c_share(via)
    for p in NEAR:
        c_copies[p].wait_recv()
        c_share(p)

    acc = epart[r]
    for i in range(1, NP):
        e_copies[i - 1].wait_recv()
        acc = acc + erecv[i]
    ehalf[...] = acc
    other = pl.ds(pl.multiple_of((1 - core) * 8, 8), 8)
    es_copy = send(ehalf.at[other], esib.at[0], es_ss.at[0], es_rs.at[0], me_other)

    for p in LEAF:
        c_copies[p].wait_recv()
        c_share(p)
    es_copy.wait_recv()
    keep = pl.ds(pl.multiple_of(core * 8, 8), 8)
    zmine[...] = ehalf[keep, :] + esib[0]
    z_copies = [
        send(zmine, zrecv.at[i], z_ss.at[i], z_rs.at[i], (r, ring(i)))
        for i in range(1, NZ)
    ]
    for copy in cs_copies:
        copy.wait_recv()

    for k in range(K):
        picked = dagg[jnp.minimum(jnp.maximum(rows[k], 0), BR - 1)]
        sums[k + 1] = dot(tiles[k], picked, down0)
    for k in range(1, K):
        sums[k + 1] = sums[k + 1] + sums[prev_c[k]]
    q_copies = []
    for i in range(NP):
        qpart[i] = sums[last_c[i]].astype(BF16)
        if i:
            q_copies.append(send(qpart.at[i], qrecv.at[i], q_ss.at[i], q_rs.at[i], (plane(i), c)))

    acc = zmine[...]
    for i in range(1, NZ):
        z_copies[i - 1].wait_recv()
        acc = acc + zrecv[i]
    fin[core] = acc
    share = send(fin.at[core], fin.at[core], es_ss.at[1], es_rs.at[1], me_other)
    share.wait_recv()
    g_copies = [
        send(fin.at[0], gwrecv.at[r], g_ss.at[i], g_rs.at[i], (plane(i), c))
        for i in range(1, NP)
    ]
    gwrecv[r] = fin[0]
    gb[...] = jnp.sum(fin[1], axis=0, keepdims=True)

    acc = qpart[0].astype(F32)
    for i in range(1, NP):
        q_copies[i - 1].wait_recv()
        acc = acc + qrecv[i].astype(F32)
    gf[...] = acc.astype(BF16)
    for copy in g_copies:
        copy.wait_recv()
    for p in range(NP):
        gw[8 * p : 8 * p + 8, :] = gwrecv[p]
    for copy in started:
        copy.wait_send()


def on_device(features, tiles, tile_rows, tile_cols, tile_count, weight, bias, cotangent):
    vmem = pl.BlockSpec(memory_space=pltpu.VMEM)
    smem = pl.BlockSpec(memory_space=pltpu.SMEM)
    hbm = pl.BlockSpec(memory_space=pl.ANY)
    dma = pltpu.SemaphoreType.DMA
    out, gf, gw, gb = pl.pallas_call(
        kernel,
        out_shape=(
            jax.ShapeDtypeStruct((T, HID), BF16),
            jax.ShapeDtypeStruct((T, T), BF16),
            jax.ShapeDtypeStruct((T, HID), F32),
            jax.ShapeDtypeStruct((1, HID), F32),
        ),
        in_specs=[hbm, hbm, smem, smem, smem, hbm, vmem, hbm],
        out_specs=(vmem,) * 4,
        scratch_shapes=[
            pltpu.VMEM((K, T, T), BF16),
            pltpu.VMEM((T, HID), F32),
            pltpu.VMEM((T, HID), BF16),
            pltpu.VMEM((NP, T, T), BF16),
            pltpu.VMEM((K + 1, T, T), F32),
            pltpu.VMEM((2, NZ, T, T), BF16),
            pltpu.VMEM((NZ, T, T), BF16),
            pltpu.VMEM((NZ, T, T), BF16),
            pltpu.VMEM((NZ, T, T), BF16),
            pltpu.VMEM((2 * NZ, T, T), BF16),
            pltpu.VMEM((NP, T, T), BF16),
            pltpu.VMEM((NP, T, T), BF16),
            pltpu.VMEM((NP, 16, HID), F32),
            pltpu.VMEM((NP, 16, HID), F32),
            pltpu.VMEM((16, HID), F32),
            pltpu.VMEM((1, 8, HID), F32),
            pltpu.VMEM((8, HID), F32),
            pltpu.VMEM((NZ, 8, HID), F32),
            pltpu.VMEM((2, 8, HID), F32),
            pltpu.VMEM((NP, 8, HID), F32),
            dma((4,)),
        ]
        + [dma((16,))] * 20,
        compiler_params=pltpu.CompilerParams(
            collective_id=0, has_side_effects=True, vmem_limit_bytes=60 * 1024 * 1024
        ),
    )(
        features,
        tiles.reshape(K, T, T),
        tile_rows.reshape(K),
        tile_cols.reshape(K),
        tile_count.reshape(1),
        weight,
        bias.reshape(1, HID),
        cotangent,
    )
    return out, gf, gw, gb.reshape(HID)


def solution(mesh):
    placed = (
        P(("col", "row"), None),
        P("row", "col", None, None, None),
        P("row", "col", None),
        P("row", "col", None),
        P("row", "col"),
        P(),
        P(),
        P(("row", "col"), None),
    )
    return jax.shard_map(
        on_device,
        mesh=mesh,
        in_specs=placed,
        out_specs=(P(("row", "col"), None), P(("col", "row"), None), P(), P()),
        check_vma=False,
    )
```

time: 763 us -> 82.1 us (0.11)
  waiting for transfers between devices: 609 us -> 0 us
  blocking collectives: 123 us -> 0 us
  Pallas kernels: 0 us -> 76.5 us
  between operations: 14.6 us -> 1.3 us
    psum x1 -> x0, waiting for transfers between devices: 344 us -> none  [on_device(): lax.psum((local_weight, local_bias), ('row', 'col'))]
    reduce_scatter x2 -> x0, waiting for transfers between devices: 193 us -> none  [the longest x1 113 us: on_device(): lax.psum_scatter(partial_value.astype(jnp.bfloat16), 'col', scatter_dimen...]
    psum x1 -> x0, blocking collectives: 103 us -> none  [on_device(): lax.psum((local_weight, local_bias), ('row', 'col'))]
    pallas_call x0 -> x1, Pallas kernels: none -> 76.5 us  [on_device(): pl.pallas_call(kernel, out_shape=(jax.ShapeDtypeStruct((T, HID), BF16), j...]
    all_gather x1 -> x0, waiting for transfers between devices: 70.9 us -> none  [on_device(): block_grads = lax.all_gather(daggregated, 'col', axis=0, tiled=True)]
    all_gather x1 -> x0, blocking collectives: 20 us -> none  [on_device(): column_feats = lax.all_gather(features, 'row', axis=0, tiled=True)]
  transfers between devices with their start and end apart: 4 -> 0, of which waited for: 4 -> 0; matrix products, arithmetic and copies ran while one was open for 1% -> 0% of each run, Pallas kernels for 0% -> 0%
where the time goes in v1:
time: 82.1 us; the launch traced here: 81.9 us
  Pallas kernels  76.5 us (93%)
  local copies, waits for them, and re-layouts  4.12 us (5%)
  between operations  1.3 us (2%)
    pallas_call x1, Pallas kernels, on_device(): pl.pallas_call(kernel, out_shape=(jax.ShapeDtypeStruct((T, HID), BF16), j...  76.5 us
    unnamed x8, local copies, waits for them, and re-layouts  4.12 us

profile of v1, /device:TPU:1, one launch (start us, length us, event | category | flops | bytes accessed | tf_op | source)
XLA Modules:
  0.0 81.9 jit_solution(10978291460388927401)
XLA Ops:
  1.3 76.5 %shard_map.111 = (bf16[128,256]{1,0:T(8,128)(2,1)}, bf16[128,128]{1,0:T(8,128)(2,1)}, f32[128,256]{1,0:T(8,128)}, f32[1,256]{1,0:T(1,128)}) custom-call(bf16[128,128]{1,0:T(8,128)(2,1)} %feat.1, bf16[16,128,128]{2,1,0:T(8,128)(2,1)} %bitcast.7, s32[16]{0:T(128)} %bitcast.10, s32[16]{0:T(128)} %bitcast.11, s32[1]{0:T(128)} %bitcast.6.count, ...), custom_call_target="tpu_custom_call" | custom-call | tf_op jit(solution)/shard_map/pallas_call | solution.py:280
  77.8 0.0 copy-start
  77.8 1.5 %copy.17 = bf16[128,256]{1,0:T(8,128)(2,1)} copy(bf16[128,256]{1,0:T(8,128)(2,1)} %get-tuple-element.16) | data formatting | bytes 131072
  79.3 1.4 %copy.18 = bf16[128,128]{1,0:T(8,128)(2,1)} copy(bf16[128,128]{1,0:T(8,128)(2,1)} %get-tuple-element.17) | data formatting | bytes 65536
  80.7 0.0 copy-done
  80.7 0.0 copy-start.1
  80.7 0.7 copy.19
  81.3 0.0 copy-done.1
  81.3 0.6 copy.20
Async XLA Ops:
  77.8 2.9 %copy-start = (f32[128,256]{1,0:T(8,128)S(1)}, f32[128,256]{1,0:T(8,128)}, u32[]{:S(2)}) copy-start(f32[128,256]{1,0:T(8,128)} %get-tuple-element.18) | copy-start | bytes 393220
  80.7 0.7 copy-start.1

commit v2 on v1

--- a/solution.py
+++ b/solution.py
@@ -21,6 +21,7 @@
 RELAY = [6, -5, 3, -2]
 NEAR = [1, -1]
 ORDER = list(LEAF) + NEAR + RELAY + [0]
+FAR_FIRST = sorted(range(1, NP), key=lambda i: -min(i // 4, 4 - i // 4) - min(i % 4, 4 - i % 4))
 AT = {p: n for n, p in enumerate(ORDER)}
 C0 = 0.7978845608028654
 C1 = 0.044715
@@ -36,13 +37,13 @@
 
 
 def kernel(
-    feat, tiles_hbm, rows, cols, count, w_hbm, bias, cot_hbm,
+    feat, tiles_hbm, rows_hbm, cols_hbm, count_hbm, w_hbm, bias_hbm, cot_hbm,
     out, gf, gw, gb,
-    tiles, w, cot, feats, sums, part, sib, bsend, brecv, dagg, qpart, qrecv,
-    epart, erecv, ehalf, esib, zmine, zrecv, fin, gwrecv,
+    rows, cols, count, tiles, w, bias, cot, feats, sums, part, sib, bsend, brecv, dagg, qpart, qrecv,
+    epart, erecv, zall, fin,
     in_sem, a_ss, a_rs, p_ss, p_rs, b_ss, b_rs,
     c_ss, c_rs, cs_ss, cs_rs, q_ss, q_rs,
-    e_ss, e_rs, es_ss, es_rs, z_ss, z_rs, g_ss, g_rs,
+    e_ss, e_rs, z_ss, z_rs, g_ss, g_rs,
 ):
     r = lax.axis_index("row")
     c = lax.axis_index("col")
@@ -56,12 +57,11 @@
         return ((z + i) % NZ) * 2 + core
 
     me_other = (r, z * 2 + 1 - core)
-    loads = [
-        pltpu.make_async_copy(a, b, in_sem.at[n])
-        for n, (a, b) in enumerate(
-            ((feat, feats.at[r]), (tiles_hbm, tiles), (w_hbm, w), (cot_hbm, cot))
-        )
-    ]
+    operands = (
+        (feat, feats.at[r]), (rows_hbm, rows), (cols_hbm, cols), (count_hbm, count),
+        (tiles_hbm, tiles), (w_hbm, w), (bias_hbm, bias), (cot_hbm, cot),
+    )
+    loads = [pltpu.make_async_copy(a, b, in_sem.at[n]) for n, (a, b) in enumerate(operands)]
     for copy in loads:
         copy.start()
     started = []
@@ -84,10 +84,11 @@
     pl.semaphore_wait(barrier, NP + NZ - 1)
 
     a_copies = [
-        send(feat, feats.at[r], a_ss.at[i], a_rs.at[i], (plane(i), c))
-        for i in range(1, NP)
+        send(feat, feats.at[r], a_ss.at[i], a_rs.at[i], (plane(i), c)) for i in FAR_FIRST
     ]
 
+    for copy in loads[1:4]:
+        copy.wait()
     live = count[0]
     dead = [NODES * jnp.minimum(jnp.maximum(k + 1 - live, 0), 1) for k in range(K)]
     slot_r = [rows[k] + dead[k] for k in range(K)]
@@ -110,7 +111,7 @@
     last_c = [latest(slot_c, K, plane(i)) for i in range(NP)]
 
     sums[0] = jnp.zeros((T, T), F32)
-    for copy in loads:
+    for copy in (loads[0], *loads[4:]):
         copy.wait()
     for copy in a_copies:
         copy.wait_recv()
@@ -123,13 +124,11 @@
     p_copies = []
     for g in range(4):
         for j in range(4 * g, 4 * g + 4):
-            part[0, j] = sums[last_r[0][j]].astype(BF16)
+            part[j] = sums[last_r[0][j]].astype(BF16)
         four = pl.ds(4 * g, 4)
         p_copies.append(
-            send(part.at[0, four], sib.at[four], p_ss.at[g], p_rs.at[g], me_other)
-        )
-    for j in range(NZ):
-        part[1, j] = sums[last_r[1][j]].astype(BF16)
+            send(part.at[four], sib.at[four], p_ss.at[g], p_rs.at[g], me_other)
+        )
 
     b_copies = {}
 
@@ -137,7 +136,7 @@
         j = AT[p]
         if j % 4 == 0:
             p_copies[j // 4].wait_recv()
-        return part[1, j].astype(F32) + sib[j].astype(F32)
+        return sums[last_r[1][j]] + sib[j].astype(F32)
 
     def pass_on(p, to):
         v = own(p)
@@ -195,12 +194,20 @@
     down0 = ((0,), (0,))
     local_w = dot(agg, dp_hi, down0) + dot(agg, dp_lo, down0)
     local_b = jnp.sum(dpre.reshape(T // 8, 8, HID), axis=0)
-    for p in range(NP):
-        epart[p, 0:8] = local_w[8 * p : 8 * p + 8]
-        epart[p, 8:16] = local_b
+    for h in range(2):
+        lanes = slice(T * h, T * h + T)
+        for p in range(NP):
+            epart[p, h, 0:8] = local_w[8 * p : 8 * p + 8, lanes]
+            epart[p, h, 8:16] = local_b[:, lanes]
+
+    cores = (core, 1 - core)
+    pairs = [(i, t) for i in FAR_FIRST + [0] for t in (0, 1) if i or t]
     e_copies = [
-        send(epart.at[plane(i)], erecv.at[i], e_ss.at[i], e_rs.at[i], (plane(i), c))
-        for i in range(1, NP)
+        send(
+            epart.at[plane(i), cores[t]], erecv.at[2 * i + t], e_ss.at[2 * i + t],
+            e_rs.at[2 * i + t], (plane(i), z * 2 + cores[t]),
+        )
+        for i, t in pairs
     ]
 
     for via in RELAY:
@@ -213,24 +220,20 @@
         c_copies[p].wait_recv()
         c_share(p)
 
-    acc = epart[r]
-    for i in range(1, NP):
-        e_copies[i - 1].wait_recv()
-        acc = acc + erecv[i]
-    ehalf[...] = acc
-    other = pl.ds(pl.multiple_of((1 - core) * 8, 8), 8)
-    es_copy = send(ehalf.at[other], esib.at[0], es_ss.at[0], es_rs.at[0], me_other)
+    for copy in e_copies:
+        copy.wait_recv()
+    acc = epart[r, core]
+    for n in range(1, 2 * NP):
+        acc = acc + erecv[n]
+    zall[z] = acc.astype(BF16)
+    z_copies = [
+        send(zall.at[z], zall.at[z], z_ss.at[i], z_rs.at[i], (r, ring(i)))
+        for i in (8, 7, 9, 6, 10, 5, 11, 4, 12, 3, 13, 2, 14, 1, 15)
+    ]
 
     for p in LEAF:
         c_copies[p].wait_recv()
         c_share(p)
-    es_copy.wait_recv()
-    keep = pl.ds(pl.multiple_of(core * 8, 8), 8)
-    zmine[...] = ehalf[keep, :] + esib[0]
-    z_copies = [
-        send(zmine, zrecv.at[i], z_ss.at[i], z_rs.at[i], (r, ring(i)))
-        for i in range(1, NZ)
-    ]
     for copy in cs_copies:
         copy.wait_recv()
 
@@ -239,78 +242,95 @@
         sums[k + 1] = dot(tiles[k], picked, down0)
     for k in range(1, K):
         sums[k + 1] = sums[k + 1] + sums[prev_c[k]]
-    q_copies = []
-    for i in range(NP):
+    q_copies = {}
+    for i in FAR_FIRST + [0]:
         qpart[i] = sums[last_c[i]].astype(BF16)
         if i:
-            q_copies.append(send(qpart.at[i], qrecv.at[i], q_ss.at[i], q_rs.at[i], (plane(i), c)))
-
-    acc = zmine[...]
+            q_copies[i] = send(
+                qpart.at[i], qrecv.at[i], q_ss.at[i], q_rs.at[i], (plane(i), c)
+            )
+    early = len(started) - NP + 1
+    for copy in started[:early]:
+        copy.wait_send()
+
+    for copy in z_copies:
+        copy.wait_recv()
+    acc = zall[0].astype(F32)
     for i in range(1, NZ):
-        z_copies[i - 1].wait_recv()
-        acc = acc + zrecv[i]
-    fin[core] = acc
-    share = send(fin.at[core], fin.at[core], es_ss.at[1], es_rs.at[1], me_other)
-    share.wait_recv()
-    g_copies = [
-        send(fin.at[0], gwrecv.at[r], g_ss.at[i], g_rs.at[i], (plane(i), c))
-        for i in range(1, NP)
-    ]
-    gwrecv[r] = fin[0]
-    gb[...] = jnp.sum(fin[1], axis=0, keepdims=True)
+        acc = acc + zall[i].astype(F32)
+    fin[r, core] = acc
+    g_copies = []
+    for i, t in pairs:
+        piece = fin.at[r, core, pl.ds(0, 8)] if i else fin.at[r, core]
+        g_copies.append(
+            send(piece, piece, g_ss.at[2 * i + t], g_rs.at[2 * i + t], (plane(i), z * 2 + cores[t]))
+        )
 
     acc = qpart[0].astype(F32)
-    for i in range(1, NP):
-        q_copies[i - 1].wait_recv()
+    for i in FAR_FIRST:
+        q_copies[i].wait_recv()
         acc = acc + qrecv[i].astype(F32)
     gf[...] = acc.astype(BF16)
     for copy in g_copies:
         copy.wait_recv()
-    for p in range(NP):
-        gw[8 * p : 8 * p + 8, :] = gwrecv[p]
-    for copy in started:
+    for h in range(2):
+        lanes = slice(T * h, T * h + T)
+        for p in range(NP):
+            gw[8 * p : 8 * p + 8, lanes] = fin[p, h, 0:8]
+        gb[:, lanes] = jnp.sum(fin[r, h, 8:16], axis=0, keepdims=True)
+    for copy in started[early:]:
         copy.wait_send()
+
+
+def write_out(*refs):
+    sem = refs[-1]
+    copies = [pltpu.make_async_copy(refs[n], refs[4 + n], sem.at[n]) for n in range(4)]
+    for copy in copies:
+        copy.start()
+    for copy in copies:
+        copy.wait()
 
 
 def on_device(features, tiles, tile_rows, tile_cols, tile_count, weight, bias, cotangent):
     vmem = pl.BlockSpec(memory_space=pltpu.VMEM)
-    smem = pl.BlockSpec(memory_space=pltpu.SMEM)
     hbm = pl.BlockSpec(memory_space=pl.ANY)
     dma = pltpu.SemaphoreType.DMA
-    out, gf, gw, gb = pl.pallas_call(
+    shapes = (
+        jax.ShapeDtypeStruct((T, HID), BF16),
+        jax.ShapeDtypeStruct((T, T), BF16),
+        jax.ShapeDtypeStruct((T, HID), F32),
+        jax.ShapeDtypeStruct((1, HID), F32),
+    )
+    results = pl.pallas_call(
         kernel,
-        out_shape=(
-            jax.ShapeDtypeStruct((T, HID), BF16),
-            jax.ShapeDtypeStruct((T, T), BF16),
-            jax.ShapeDtypeStruct((T, HID), F32),
-            jax.ShapeDtypeStruct((1, HID), F32),
-        ),
-        in_specs=[hbm, hbm, smem, smem, smem, hbm, vmem, hbm],
+        out_shape=shapes,
+        in_specs=[hbm] * 8,
         out_specs=(vmem,) * 4,
         scratch_shapes=[
+            pltpu.SMEM((K,), jnp.int32),
+            pltpu.SMEM((K,), jnp.int32),
+            pltpu.SMEM((1,), jnp.int32),
             pltpu.VMEM((K, T, T), BF16),
             pltpu.VMEM((T, HID), F32),
+            pltpu.VMEM((1, HID), F32),
             pltpu.VMEM((T, HID), BF16),
             pltpu.VMEM((NP, T, T), BF16),
             pltpu.VMEM((K + 1, T, T), F32),
-            pltpu.VMEM((2, NZ, T, T), BF16),
+            pltpu.VMEM((NZ, T, T), BF16),
             pltpu.VMEM((NZ, T, T), BF16),
             pltpu.VMEM((NZ, T, T), BF16),
             pltpu.VMEM((NZ, T, T), BF16),
             pltpu.VMEM((2 * NZ, T, T), BF16),
             pltpu.VMEM((NP, T, T), BF16),
             pltpu.VMEM((NP, T, T), BF16),
-            pltpu.VMEM((NP, 16, HID), F32),
-            pltpu.VMEM((NP, 16, HID), F32),
-            pltpu.VMEM((16, HID), F32),
-            pltpu.VMEM((1, 8, HID), F32),
-            pltpu.VMEM((8, HID), F32),
-            pltpu.VMEM((NZ, 8, HID), F32),
-            pltpu.VMEM((2, 8, HID), F32),
-            pltpu.VMEM((NP, 8, HID), F32),
-            dma((4,)),
+            pltpu.VMEM((NP, 2, 16, T), F32),
+            pltpu.VMEM((2 * NP, 16, T), F32),
+            pltpu.VMEM((NZ, 16, T), BF16),
+            pltpu.VMEM((NP, 2, 16, T), F32),
+            dma((8,)),
         ]
-        + [dma((16,))] * 20,
+        + [dma((16,))] * 12
+        + [dma((32,)), dma((32,)), dma((16,)), dma((16,)), dma((32,)), dma((32,))],
         compiler_params=pltpu.CompilerParams(
             collective_id=0, has_side_effects=True, vmem_limit_bytes=60 * 1024 * 1024
         ),
@@ -324,6 +344,13 @@
         bias.reshape(1, HID),
         cotangent,
     )
+    out, gf, gw, gb = pl.pallas_call(
+        write_out,
+        out_shape=shapes,
+        in_specs=[vmem] * 4,
+        out_specs=(hbm,) * 4,
+        scratch_shapes=[dma((4,))],
+    )(*results)
     return out, gf, gw, gb.reshape(HID)
 
 

time: 82.1 us -> 76.8 us (0.935)
  local copies, waits for them, and re-layouts: 4.12 us -> 0 us
  Pallas kernels: 76.5 us -> 75.3 us
    unnamed x8 -> x0, local copies, waits for them, and re-layouts: 4.12 us -> none
    pallas_call x1 -> x2, Pallas kernels: 76.5 us -> 75.3 us  [the longest x1 73.6 us: on_device(): pl.pallas_call(kernel, out_shape=shapes, in_specs=[hbm] * 8, out_specs=(v...]
where the time goes in v2:
time: 76.8 us; the launch traced here: 76.6 us
  Pallas kernels  75.3 us (98%)
  between operations  1.29 us (2%)
    pallas_call x1, Pallas kernels, on_device(): pl.pallas_call(kernel, out_shape=shapes, in_specs=[hbm] * 8, out_specs=(v...  73.6 us
    pallas_call x1, Pallas kernels, on_device(): pl.pallas_call(write_out, out_shape=shapes, in_specs=[vmem] * 4, out_spec...  1.69 us

profile of v2, /device:TPU:1, one launch (start us, length us, event | category | flops | bytes accessed | tf_op | source)
XLA Modules:
  0.0 76.6 jit_solution(5261524304724214293)
XLA Ops:
  1.3 73.6 %shard_map.111 = (bf16[128,256]{1,0:T(8,128)(2,1)}, bf16[128,128]{1,0:T(8,128)(2,1)}, f32[128,256]{1,0:T(8,128)}, f32[1,256]{1,0:T(1,128)}) custom-call(bf16[128,128]{1,0:T(8,128)(2,1)} %feat.1, bf16[16,128,128]{2,1,0:T(8,128)(2,1)} %bitcast.7, s32[16]{0:T(128)} %bitcast.9, s32[16]{0:T(128)} %bitcast.10, s32[1]{0:T(128)} %bitcast.6.count_hbm, ...), custom_call_target="tpu_custom_call" | custom-call | tf_op jit(solution)/shard_map/pallas_call | solution.py:304
  74.9 1.7 %shard_map.112 = (bf16[128,256]{1,0:T(8,128)(2,1)}, bf16[128,128]{1,0:T(8,128)(2,1)}, f32[128,256]{1,0:T(8,128)}, f32[1,256]{1,0:T(1,128)}) custom-call(bf16[128,256]{1,0:T(8,128)(2,1)} %get-tuple-element.12.refs_0_, bf16[128,128]{1,0:T(8,128)(2,1)} %get-tuple-element.13.refs_1_, f32[128,256]{1,0:T(8,128)} %get-tuple-element.14.refs_2_, ...), custom_call_target="tpu_custom_call" | custom-call | tf_op jit(solution)/shard_map/pallas_call | solution.py:347

commit v3 on v2

--- a/solution.py
+++ b/solution.py
@@ -64,16 +64,16 @@
     loads = [pltpu.make_async_copy(a, b, in_sem.at[n]) for n, (a, b) in enumerate(operands)]
     for copy in loads:
         copy.start()
-    started = []
-
     def send(src, dst, ssem, rsem, where):
         copy = pltpu.make_async_remote_copy(
             src_ref=src, dst_ref=dst, send_sem=ssem, recv_sem=rsem,
             device_id=where, device_id_type=MESH,
         )
         copy.start()
-        started.append(copy)
         return copy
+
+    def wait(ref, sem):
+        pltpu.make_async_copy(ref, ref, sem.at[0]).wait()
 
     barrier = pltpu.get_barrier_semaphore()
     for i in range(1, NP):
@@ -83,9 +83,8 @@
     pl.semaphore_signal(barrier, inc=1, device_id=me_other, device_id_type=MESH)
     pl.semaphore_wait(barrier, NP + NZ - 1)
 
-    a_copies = [
-        send(feat, feats.at[r], a_ss.at[i], a_rs.at[i], (plane(i), c)) for i in FAR_FIRST
-    ]
+    for i in FAR_FIRST:
+        send(feat, feats.at[r], a_ss.at[0], a_rs.at[0], (plane(i), c))
 
     for copy in loads[1:4]:
         copy.wait()
@@ -113,8 +112,7 @@
     sums[0] = jnp.zeros((T, T), F32)
     for copy in (loads[0], *loads[4:]):
         copy.wait()
-    for copy in a_copies:
-        copy.wait_recv()
+    wait(feats.at[pl.ds(0, NP - 1)], a_rs)
 
     for k in range(K):
         sums[k + 1] = dot(tiles[k], feats[jnp.minimum(jnp.maximum(cols[k], 0), NP - 1)])
@@ -127,7 +125,7 @@
             part[j] = sums[last_r[0][j]].astype(BF16)
         four = pl.ds(4 * g, 4)
         p_copies.append(
-            send(part.at[four], sib.at[four], p_ss.at[g], p_rs.at[g], me_other)
+            send(part.at[four], sib.at[four], p_ss.at[0], p_rs.at[g], me_other)
         )
 
     b_copies = {}
@@ -140,14 +138,17 @@
 
     def pass_on(p, to):
         v = own(p)
-        for leaf, relay in LEAF.items():
-            if relay == p:
-                b_copies[leaf].wait_recv()
-                v = v + brecv[AT[leaf]].astype(F32)
+        leaves = [AT[leaf] for leaf, relay in LEAF.items() if relay == p]
+        if leaves:
+            held = brecv.at[pl.ds(leaves[0], len(leaves))]
+            pltpu.make_async_copy(held, held, b_rs.at[RELAY.index(p)]).wait()
+        for n in leaves:
+            v = v + brecv[n].astype(F32)
         n = AT[p]
         bsend[n] = v.astype(BF16)
         b_copies[p] = send(
-            bsend.at[n], brecv.at[n], b_ss.at[n], b_rs.at[n], (r, ring(NZ + to - p))
+            bsend.at[n], brecv.at[n], b_ss.at[0],
+            b_rs.at[RELAY.index(to) if to else n - len(LEAF) + 4], (r, ring(NZ + to - p)),
         )
 
     for p in ORDER[:-1]:
@@ -176,15 +177,12 @@
         block = dagg.at[ring(NZ - via)]
         n = AT[p]
         c_copies[p] = send(
-            block, block, c_ss.at[n], c_rs.at[n], (r, ring(NZ + p - via))
-        )
-
-    cs_copies = []
+            block, block, c_ss.at[0], c_rs.at[n], (r, ring(NZ + p - via))
+        )
 
     def c_share(p):
         block = dagg.at[ring(NZ - p)]
-        n = AT[p]
-        cs_copies.append(send(block, block, cs_ss.at[n], cs_rs.at[n], me_other))
+        send(block, block, cs_ss.at[0], cs_rs.at[0], me_other)
 
     for p in RELAY + NEAR:
         c_send(p, 0)
@@ -197,18 +195,16 @@
     for h in range(2):
         lanes = slice(T * h, T * h + T)
         for p in range(NP):
-            epart[p, h, 0:8] = local_w[8 * p : 8 * p + 8, lanes]
-            epart[p, h, 8:16] = local_b[:, lanes]
+            piece = (local_w[8 * p : 8 * p + 8, lanes], local_b[:, lanes])
+            epart[p, h] = jnp.concatenate(piece, axis=0).astype(BF16)
 
     cores = (core, 1 - core)
     pairs = [(i, t) for i in FAR_FIRST + [0] for t in (0, 1) if i or t]
-    e_copies = [
+    for i, t in pairs:
         send(
-            epart.at[plane(i), cores[t]], erecv.at[2 * i + t], e_ss.at[2 * i + t],
-            e_rs.at[2 * i + t], (plane(i), z * 2 + cores[t]),
-        )
-        for i, t in pairs
-    ]
+            epart.at[plane(i), cores[t]], erecv.at[2 * i + t], e_ss.at[0], e_rs.at[0],
+            (plane(i), z * 2 + cores[t]),
+        )
 
     for via in RELAY:
         c_copies[via].wait_recv()
@@ -220,22 +216,18 @@
         c_copies[p].wait_recv()
         c_share(p)
 
-    for copy in e_copies:
-        copy.wait_recv()
-    acc = epart[r, core]
+    wait(erecv.at[pl.ds(1, 2 * NP - 1)], e_rs)
+    acc = epart[r, core].astype(F32)
     for n in range(1, 2 * NP):
-        acc = acc + erecv[n]
+        acc = acc + erecv[n].astype(F32)
     zall[z] = acc.astype(BF16)
-    z_copies = [
-        send(zall.at[z], zall.at[z], z_ss.at[i], z_rs.at[i], (r, ring(i)))
-        for i in (8, 7, 9, 6, 10, 5, 11, 4, 12, 3, 13, 2, 14, 1, 15)
-    ]
+    for i in (8, 7, 9, 6, 10, 5, 11, 4, 12, 3, 13, 2, 14, 1, 15):
+        send(zall.at[z], zall.at[z], z_ss.at[0], z_rs.at[0], (r, ring(i)))
 
     for p in LEAF:
         c_copies[p].wait_recv()
         c_share(p)
-    for copy in cs_copies:
-        copy.wait_recv()
+    wait(dagg.at[pl.ds(0, NZ)], cs_rs)
 
     for k in range(K):
         picked = dagg[jnp.minimum(jnp.maximum(rows[k], 0), BR - 1)]
@@ -247,39 +239,38 @@
         qpart[i] = sums[last_c[i]].astype(BF16)
         if i:
             q_copies[i] = send(
-                qpart.at[i], qrecv.at[i], q_ss.at[i], q_rs.at[i], (plane(i), c)
+                qpart.at[i], qrecv.at[i], q_ss.at[0], q_rs.at[i], (plane(i), c)
             )
-    early = len(started) - NP + 1
-    for copy in started[:early]:
-        copy.wait_send()
-
-    for copy in z_copies:
-        copy.wait_recv()
+    wait(feats.at[pl.ds(0, NP - 1)], a_ss)
+    wait(part, p_ss)
+    wait(bsend.at[pl.ds(0, NZ - 1)], b_ss)
+    wait(dagg.at[pl.ds(0, NZ - 1)], c_ss)
+    wait(dagg.at[pl.ds(0, NZ)], cs_ss)
+    wait(erecv.at[pl.ds(1, 2 * NP - 1)], e_ss)
+
+    wait(zall.at[pl.ds(0, NZ - 1)], z_rs)
     acc = zall[0].astype(F32)
     for i in range(1, NZ):
         acc = acc + zall[i].astype(F32)
     fin[r, core] = acc
-    g_copies = []
     for i, t in pairs:
         piece = fin.at[r, core, pl.ds(0, 8)] if i else fin.at[r, core]
-        g_copies.append(
-            send(piece, piece, g_ss.at[2 * i + t], g_rs.at[2 * i + t], (plane(i), z * 2 + cores[t]))
-        )
+        send(piece, piece, g_ss.at[0], g_rs.at[0], (plane(i), z * 2 + cores[t]))
+    wait(zall.at[pl.ds(0, NZ - 1)], z_ss)
 
     acc = qpart[0].astype(F32)
     for i in FAR_FIRST:
         q_copies[i].wait_recv()
         acc = acc + qrecv[i].astype(F32)
     gf[...] = acc.astype(BF16)
-    for copy in g_copies:
-        copy.wait_recv()
+    wait(fin.at[pl.ds(0, NP // 2)], g_rs)
     for h in range(2):
         lanes = slice(T * h, T * h + T)
         for p in range(NP):
             gw[8 * p : 8 * p + 8, lanes] = fin[p, h, 0:8]
         gb[:, lanes] = jnp.sum(fin[r, h, 8:16], axis=0, keepdims=True)
-    for copy in started[early:]:
-        copy.wait_send()
+    wait(qrecv.at[pl.ds(0, NP - 1)], q_ss)
+    wait(fin.at[pl.ds(0, NP // 2)], g_ss)
 
 
 def write_out(*refs):
@@ -323,14 +314,12 @@
             pltpu.VMEM((2 * NZ, T, T), BF16),
             pltpu.VMEM((NP, T, T), BF16),
             pltpu.VMEM((NP, T, T), BF16),
-            pltpu.VMEM((NP, 2, 16, T), F32),
-            pltpu.VMEM((2 * NP, 16, T), F32),
+            pltpu.VMEM((NP, 2, 16, T), BF16),
+            pltpu.VMEM((2 * NP, 16, T), BF16),
             pltpu.VMEM((NZ, 16, T), BF16),
             pltpu.VMEM((NP, 2, 16, T), F32),
-            dma((8,)),
         ]
-        + [dma((16,))] * 12
-        + [dma((32,)), dma((32,)), dma((16,)), dma((16,)), dma((32,)), dma((32,))],
+        + [dma((n,)) for n in (8, 1, 1, 1, 4, 1, 10, 1, 15, 1, 1, 1, 16, 1, 1, 1, 1, 1, 1)],
         compiler_params=pltpu.CompilerParams(
             collective_id=0, has_side_effects=True, vmem_limit_bytes=60 * 1024 * 1024
         ),

time: 76.8 us -> 74.3 us (0.967)
  Pallas kernels: 75.3 us -> 72.9 us
    pallas_call x1, Pallas kernels: 73.6 us -> 71.2 us  [on_device(): pl.pallas_call(kernel, out_shape=shapes, in_specs=[hbm] * 8, out_specs=(v...]
where the time goes in v3:
time: 74.3 us; the launch traced here: 74.2 us
  Pallas kernels  72.9 us (98%)
  between operations  1.29 us (2%)
    pallas_call x1, Pallas kernels, on_device(): pl.pallas_call(kernel, out_shape=shapes, in_specs=[hbm] * 8, out_specs=(v...  71.2 us
    pallas_call x1, Pallas kernels, on_device(): pl.pallas_call(write_out, out_shape=shapes, in_specs=[vmem] * 4, out_spec...  1.69 us

profile of v3, /device:TPU:1, one launch (start us, length us, event | category | flops | bytes accessed | tf_op | source)
XLA Modules:
  0.0 74.2 jit_solution(10769865561734635493)
XLA Ops:
  1.3 71.2 %shard_map.111 = (bf16[128,256]{1,0:T(8,128)(2,1)}, bf16[128,128]{1,0:T(8,128)(2,1)}, f32[128,256]{1,0:T(8,128)}, f32[1,256]{1,0:T(1,128)}) custom-call(bf16[128,128]{1,0:T(8,128)(2,1)} %feat.1, bf16[16,128,128]{2,1,0:T(8,128)(2,1)} %bitcast.7, s32[16]{0:T(128)} %bitcast.9, s32[16]{0:T(128)} %bitcast.10, s32[1]{0:T(128)} %bitcast.6.count_hbm, ...), custom_call_target="tpu_custom_call" | custom-call | tf_op jit(solution)/shard_map/pallas_call | solution.py:295
  72.5 1.7 %shard_map.112 = (bf16[128,256]{1,0:T(8,128)(2,1)}, bf16[128,128]{1,0:T(8,128)(2,1)}, f32[128,256]{1,0:T(8,128)}, f32[1,256]{1,0:T(1,128)}) custom-call(bf16[128,256]{1,0:T(8,128)(2,1)} %get-tuple-element.12.refs_0_, bf16[128,128]{1,0:T(8,128)(2,1)} %get-tuple-element.13.refs_1_, f32[128,256]{1,0:T(8,128)} %get-tuple-element.14.refs_2_, ...), custom_call_target="tpu_custom_call" | custom-call | tf_op jit(solution)/shard_map/pallas_call | solution.py:336

commit v4 on v3

--- a/solution.py
+++ b/solution.py
@@ -17,8 +17,8 @@
 BR = 32
 NODES = 65536
 HID = 256
-LEAF = {5: 6, 7: 6, 8: 6, -4: -5, -6: -5, -7: -5, 2: 3, 4: 3, -3: -2}
-RELAY = [6, -5, 3, -2]
+LEAF = {8: 5, 7: 5, 6: 5, 4: 5, -7: -5, -6: -5, -4: -5, 3: 2, -3: -2}
+RELAY = [5, -5, 2, -2]
 NEAR = [1, -1]
 ORDER = list(LEAF) + NEAR + RELAY + [0]
 FAR_FIRST = sorted(range(1, NP), key=lambda i: -min(i // 4, 4 - i // 4) - min(i % 4, 4 - i % 4))
@@ -216,17 +216,18 @@
         c_copies[p].wait_recv()
         c_share(p)
 
-    wait(erecv.at[pl.ds(1, 2 * NP - 1)], e_rs)
-    acc = epart[r, core].astype(F32)
-    for n in range(1, 2 * NP):
-        acc = acc + erecv[n].astype(F32)
-    zall[z] = acc.astype(BF16)
-    for i in (8, 7, 9, 6, 10, 5, 11, 4, 12, 3, 13, 2, 14, 1, 15):
-        send(zall.at[z], zall.at[z], z_ss.at[0], z_rs.at[0], (r, ring(i)))
-
-    for p in LEAF:
+    for turn, p in enumerate(LEAF):
         c_copies[p].wait_recv()
         c_share(p)
+        if turn == 3:
+            wait(erecv.at[pl.ds(1, 2 * NP - 1)], e_rs)
+            acc = epart[r, core].astype(F32)
+            for n in range(1, 2 * NP):
+                acc = acc + erecv[n].astype(F32)
+            zall[z] = acc.astype(BF16)
+            for i in (8, 7, 9, 6, 10, 5, 11, 4, 12, 3, 13, 2, 14, 1, 15):
+                send(zall.at[z], zall.at[z], z_ss.at[0], z_rs.at[0], (r, ring(i)))
+
     wait(dagg.at[pl.ds(0, NZ)], cs_rs)
 
     for k in range(K):

time: 74.3 us -> 71.8 us (0.966)
  Pallas kernels: 72.9 us -> 70.3 us
    pallas_call x1, Pallas kernels: 71.2 us -> 68.7 us  [on_device(): pl.pallas_call(kernel, out_shape=shapes, in_specs=[hbm] * 8, out_specs=(v...]
where the time goes in v4:
time: 71.8 us; the launch traced here: 71.6 us
  Pallas kernels  70.3 us (98%)
  between operations  1.29 us (2%)
    pallas_call x1, Pallas kernels, on_device(): pl.pallas_call(kernel, out_shape=shapes, in_specs=[hbm] * 8, out_specs=(v...  68.7 us
    pallas_call x1, Pallas kernels, on_device(): pl.pallas_call(write_out, out_shape=shapes, in_specs=[vmem] * 4, out_spec...  1.69 us

profile of v4, /device:TPU:1, one launch (start us, length us, event | category | flops | bytes accessed | tf_op | source)
XLA Modules:
  0.0 71.6 jit_solution(14421180289929222373)
XLA Ops:
  1.3 68.7 %shard_map.111 = (bf16[128,256]{1,0:T(8,128)(2,1)}, bf16[128,128]{1,0:T(8,128)(2,1)}, f32[128,256]{1,0:T(8,128)}, f32[1,256]{1,0:T(1,128)}) custom-call(bf16[128,128]{1,0:T(8,128)(2,1)} %feat.1, bf16[16,128,128]{2,1,0:T(8,128)(2,1)} %bitcast.7, s32[16]{0:T(128)} %bitcast.9, s32[16]{0:T(128)} %bitcast.10, s32[1]{0:T(128)} %bitcast.6.count_hbm, ...), custom_call_target="tpu_custom_call" | custom-call | tf_op jit(solution)/shard_map/pallas_call | solution.py:296
  69.9 1.7 %shard_map.112 = (bf16[128,256]{1,0:T(8,128)(2,1)}, bf16[128,128]{1,0:T(8,128)(2,1)}, f32[128,256]{1,0:T(8,128)}, f32[1,256]{1,0:T(1,128)}) custom-call(bf16[128,256]{1,0:T(8,128)(2,1)} %get-tuple-element.12.refs_0_, bf16[128,128]{1,0:T(8,128)(2,1)} %get-tuple-element.13.refs_1_, f32[128,256]{1,0:T(8,128)} %get-tuple-element.14.refs_2_, ...), custom_call_target="tpu_custom_call" | custom-call | tf_op jit(solution)/shard_map/pallas_call | solution.py:337

commit v5 on v4

--- a/solution.py
+++ b/solution.py
@@ -39,7 +39,7 @@
 def kernel(
     feat, tiles_hbm, rows_hbm, cols_hbm, count_hbm, w_hbm, bias_hbm, cot_hbm,
     out, gf, gw, gb,
-    rows, cols, count, tiles, w, bias, cot, feats, sums, part, sib, bsend, brecv, dagg, qpart, qrecv,
+    rows, cols, count, tiles, w, bias, cot, feats, sums, part, sib, wsplit, bsend, brecv, dagg, qpart, qrecv,
     epart, erecv, zall, fin,
     in_sem, a_ss, a_rs, p_ss, p_rs, b_ss, b_rs,
     c_ss, c_rs, cs_ss, cs_rs, q_ss, q_rs,
@@ -128,70 +128,81 @@
             send(part.at[four], sib.at[four], p_ss.at[0], p_rs.at[g], me_other)
         )
 
+    halves = (pl.ds(0, T // 2), pl.ds(T // 2, T // 2))
+    signs = (1, -1)
     b_copies = {}
-
-    def own(p):
-        j = AT[p]
-        if j % 4 == 0:
+    waited = set()
+
+    def own(h, p):
+        j = AT[(signs[h] * p + 7) % NZ - 7]
+        if j // 4 not in waited:
             p_copies[j // 4].wait_recv()
-        return sums[last_r[1][j]] + sib[j].astype(F32)
-
-    def pass_on(p, to):
-        v = own(p)
+            waited.add(j // 4)
+        return sums[last_r[1][j], halves[h]] + sib[j, halves[h]].astype(F32)
+
+    def pass_on(h, p, to):
+        v = own(h, p)
         leaves = [AT[leaf] for leaf, relay in LEAF.items() if relay == p]
         if leaves:
-            held = brecv.at[pl.ds(leaves[0], len(leaves))]
-            pltpu.make_async_copy(held, held, b_rs.at[RELAY.index(p)]).wait()
+            held = brecv.at[pl.ds(leaves[0], len(leaves)), halves[h]]
+            pltpu.make_async_copy(held, held, b_rs.at[10 * h + RELAY.index(p)]).wait()
         for n in leaves:
-            v = v + brecv[n].astype(F32)
+            v = v + brecv[n, halves[h]].astype(F32)
         n = AT[p]
-        bsend[n] = v.astype(BF16)
-        b_copies[p] = send(
-            bsend.at[n], brecv.at[n], b_ss.at[0],
-            b_rs.at[RELAY.index(to) if to else n - len(LEAF) + 4], (r, ring(NZ + to - p)),
-        )
-
-    for p in ORDER[:-1]:
-        pass_on(p, LEAF.get(p, 0))
-    total = own(0)
-    for p in NEAR + RELAY:
-        b_copies[p].wait_recv()
-        total = total + brecv[AT[p]].astype(F32)
-    agg = total.astype(BF16)
-
+        bsend[n, halves[h]] = v.astype(BF16)
+        b_copies[h, p] = send(
+            bsend.at[n, halves[h]], brecv.at[n, halves[h]], b_ss.at[0],
+            b_rs.at[10 * h + (RELAY.index(to) if to else n - len(LEAF) + 4)],
+            (r, ring(NZ + signs[h] * (to - p))),
+        )
+
+    for h in range(2):
+        for p in list(LEAF) + NEAR:
+            pass_on(h, p, LEAF.get(p, 0))
     w_hi, w_lo = split(w[...])
-    pre = dot(agg, w_hi) + dot(agg, w_lo) + bias[...]
-    square = pre * pre
-    t = jnp.tanh(C0 * (pre + C1 * (square * pre)))
-    half = 0.5 * (1.0 + t)
-    slope = half + 0.5 * pre * (1.0 - t * t) * (C0 * (1.0 + 3.0 * C1 * square))
-    dpre = cot[...].astype(F32) * slope
-    dp_hi, dp_lo = split(dpre)
-    back = ((1,), (1,))
-    da = dot(dp_hi, w_hi, back) + dot(dp_lo, w_hi, back) + dot(dp_hi, w_lo, back)
-    dagg[c] = da.astype(BF16)
+    wsplit[0] = w_hi
+    wsplit[1] = w_lo
+    for h in range(2):
+        for p in RELAY:
+            pass_on(h, p, 0)
 
     c_copies = {}
 
-    def c_send(p, via):
-        block = dagg.at[ring(NZ - via)]
-        n = AT[p]
-        c_copies[p] = send(
-            block, block, c_ss.at[0], c_rs.at[n], (r, ring(NZ + p - via))
-        )
-
-    def c_share(p):
-        block = dagg.at[ring(NZ - p)]
+    def c_send(h, p, via):
+        block = dagg.at[ring(NZ - signs[h] * via), halves[h]]
+        c_copies[h, p] = send(
+            block, block, c_ss.at[0], c_rs.at[15 * h + AT[p]], (r, ring(NZ + signs[h] * (p - via)))
+        )
+
+    def c_share(h, p):
+        block = dagg.at[ring(NZ - signs[h] * p), halves[h]]
         send(block, block, cs_ss.at[0], cs_rs.at[0], me_other)
 
-    for p in RELAY + NEAR:
-        c_send(p, 0)
-    c_share(0)
-
-    out[...] = (pre * half).astype(BF16)
-    down0 = ((0,), (0,))
-    local_w = dot(agg, dp_hi, down0) + dot(agg, dp_lo, down0)
-    local_b = jnp.sum(dpre.reshape(T // 8, 8, HID), axis=0)
+    back, down0 = ((1,), (1,)), ((0,), (0,))
+    local_w = local_b = 0.0
+    for h in range(2):
+        total = own(h, 0)
+        for p in NEAR + RELAY:
+            b_copies[h, p].wait_recv()
+            total = total + brecv[AT[p], halves[h]].astype(F32)
+        agg = total.astype(BF16)
+        w_hi, w_lo = wsplit[0], wsplit[1]
+        pre = dot(agg, w_hi) + dot(agg, w_lo) + bias[...]
+        square = pre * pre
+        t = jnp.tanh(C0 * (pre + C1 * (square * pre)))
+        half = 0.5 * (1.0 + t)
+        slope = half + 0.5 * pre * (1.0 - t * t) * (C0 * (1.0 + 3.0 * C1 * square))
+        dpre = cot[halves[h], :].astype(F32) * slope
+        dp_hi, dp_lo = split(dpre)
+        da = dot(dp_hi, w_hi, back) + dot(dp_lo, w_hi, back) + dot(dp_hi, w_lo, back)
+        dagg[c, halves[h]] = da.astype(BF16)
+        for p in RELAY + NEAR:
+            c_send(h, p, 0)
+        c_share(h, 0)
+        out[halves[h], :] = (pre * half).astype(BF16)
+        local_w = local_w + dot(agg, dp_hi, down0) + dot(agg, dp_lo, down0)
+        local_b = local_b + jnp.sum(dpre.reshape(T // 16, 8, HID), axis=0)
+
     for h in range(2):
         lanes = slice(T * h, T * h + T)
         for p in range(NP):
@@ -206,20 +217,21 @@
             (plane(i), z * 2 + cores[t]),
         )
 
-    for via in RELAY:
-        c_copies[via].wait_recv()
-        for p, relay in LEAF.items():
-            if relay == via:
-                c_send(p, via)
-        c_share(via)
-    for p in NEAR:
-        c_copies[p].wait_recv()
-        c_share(p)
-
-    for turn, p in enumerate(LEAF):
-        c_copies[p].wait_recv()
-        c_share(p)
-        if turn == 3:
+    for h in range(2):
+        for via in RELAY:
+            c_copies[h, via].wait_recv()
+            for p, relay in LEAF.items():
+                if relay == via:
+                    c_send(h, p, via)
+            c_share(h, via)
+        for p in NEAR:
+            c_copies[h, p].wait_recv()
+            c_share(h, p)
+
+    for turn, (h, p) in enumerate((h, p) for h in range(2) for p in LEAF):
+        c_copies[h, p].wait_recv()
+        c_share(h, p)
+        if turn == 12:
             wait(erecv.at[pl.ds(1, 2 * NP - 1)], e_rs)
             acc = epart[r, core].astype(F32)
             for n in range(1, 2 * NP):
@@ -310,6 +322,7 @@
             pltpu.VMEM((K + 1, T, T), F32),
             pltpu.VMEM((NZ, T, T), BF16),
             pltpu.VMEM((NZ, T, T), BF16),
+            pltpu.VMEM((2, T, HID), BF16),
             pltpu.VMEM((NZ, T, T), BF16),
             pltpu.VMEM((NZ, T, T), BF16),
             pltpu.VMEM((2 * NZ, T, T), BF16),
@@ -320,7 +333,7 @@
             pltpu.VMEM((NZ, 16, T), BF16),
             pltpu.VMEM((NP, 2, 16, T), F32),
         ]
-        + [dma((n,)) for n in (8, 1, 1, 1, 4, 1, 10, 1, 15, 1, 1, 1, 16, 1, 1, 1, 1, 1, 1)],
+        + [dma((n,)) for n in (8, 1, 1, 1, 4, 1, 20, 1, 30, 1, 1, 1, 16, 1, 1, 1, 1, 1, 1)],
         compiler_params=pltpu.CompilerParams(
             collective_id=0, has_side_effects=True, vmem_limit_bytes=60 * 1024 * 1024
         ),

time: 71.8 us -> 68.7 us (0.957)
  Pallas kernels: 70.3 us -> 67.3 us
    pallas_call x1, Pallas kernels: 68.7 us -> 65.6 us  [on_device(): pl.pallas_call(kernel, out_shape=shapes, in_specs=[hbm] * 8, out_specs=(v...]
where the time goes in v5:
time: 68.7 us; the launch traced here: 68.6 us
  Pallas kernels  67.3 us (98%)
  between operations  1.29 us (2%)
    pallas_call x1, Pallas kernels, on_device(): pl.pallas_call(kernel, out_shape=shapes, in_specs=[hbm] * 8, out_specs=(v...  65.6 us
    pallas_call x1, Pallas kernels, on_device(): pl.pallas_call(write_out, out_shape=shapes, in_specs=[vmem] * 4, out_spec...  1.69 us

profile of v5, /device:TPU:1, one launch (start us, length us, event | category | flops | bytes accessed | tf_op | source)
XLA Modules:
  0.0 68.6 jit_solution(14835119610579364257)
XLA Ops:
  1.3 65.6 %shard_map.111 = (bf16[128,256]{1,0:T(8,128)(2,1)}, bf16[128,128]{1,0:T(8,128)(2,1)}, f32[128,256]{1,0:T(8,128)}, f32[1,256]{1,0:T(1,128)}) custom-call(bf16[128,128]{1,0:T(8,128)(2,1)} %feat.1, bf16[16,128,128]{2,1,0:T(8,128)(2,1)} %bitcast.7, s32[16]{0:T(128)} %bitcast.9, s32[16]{0:T(128)} %bitcast.10, s32[1]{0:T(128)} %bitcast.6.count_hbm, ...), custom_call_target="tpu_custom_call" | custom-call | tf_op jit(solution)/shard_map/pallas_call | solution.py:308
  66.9 1.7 %shard_map.112 = (bf16[128,256]{1,0:T(8,128)(2,1)}, bf16[128,128]{1,0:T(8,128)(2,1)}, f32[128,256]{1,0:T(8,128)}, f32[1,256]{1,0:T(1,128)}) custom-call(bf16[128,256]{1,0:T(8,128)(2,1)} %get-tuple-element.12.refs_0_, bf16[128,128]{1,0:T(8,128)(2,1)} %get-tuple-element.13.refs_1_, f32[128,256]{1,0:T(8,128)} %get-tuple-element.14.refs_2_, ...), custom_call_target="tpu_custom_call" | custom-call | tf_op jit(solution)/shard_map/pallas_call | solution.py:350

commit v6 on v5

--- a/solution.py
+++ b/solution.py
@@ -23,6 +23,7 @@
 ORDER = list(LEAF) + NEAR + RELAY + [0]
 FAR_FIRST = sorted(range(1, NP), key=lambda i: -min(i // 4, 4 - i // 4) - min(i % 4, 4 - i % 4))
 AT = {p: n for n, p in enumerate(ORDER)}
+ZNEAR = [1, 2, 3, 5, 11, 13, 14, 15]
 C0 = 0.7978845608028654
 C1 = 0.044715
 
@@ -78,10 +79,10 @@
     barrier = pltpu.get_barrier_semaphore()
     for i in range(1, NP):
         pl.semaphore_signal(barrier, inc=1, device_id=(plane(i), c), device_id_type=MESH)
-    for i in range(1, NZ):
+    for i in ZNEAR:
         pl.semaphore_signal(barrier, inc=1, device_id=(r, ring(i)), device_id_type=MESH)
     pl.semaphore_signal(barrier, inc=1, device_id=me_other, device_id_type=MESH)
-    pl.semaphore_wait(barrier, NP + NZ - 1)
+    pl.semaphore_wait(barrier, NP + len(ZNEAR))
 
     for i in FAR_FIRST:
         send(feat, feats.at[r], a_ss.at[0], a_rs.at[0], (plane(i), c))
@@ -179,7 +180,7 @@
         send(block, block, cs_ss.at[0], cs_rs.at[0], me_other)
 
     back, down0 = ((1,), (1,)), ((0,), (0,))
-    local_w = local_b = 0.0
+    kept = []
     for h in range(2):
         total = own(h, 0)
         for p in NEAR + RELAY:
@@ -200,9 +201,12 @@
             c_send(h, p, 0)
         c_share(h, 0)
         out[halves[h], :] = (pre * half).astype(BF16)
+        kept.append((agg, dp_hi, dp_lo, dpre))
+
+    local_w = local_b = 0.0
+    for agg, dp_hi, dp_lo, dpre in kept:
         local_w = local_w + dot(agg, dp_hi, down0) + dot(agg, dp_lo, down0)
         local_b = local_b + jnp.sum(dpre.reshape(T // 16, 8, HID), axis=0)
-
     for h in range(2):
         lanes = slice(T * h, T * h + T)
         for p in range(NP):
@@ -228,17 +232,25 @@
             c_copies[h, p].wait_recv()
             c_share(h, p)
 
+    z_copies = {}
+
+    def z_send(p, via):
+        slot = zall.at[(z + NZ - via) % NZ]
+        z_copies[p] = send(
+            slot, slot, z_ss.at[0], z_rs.at[AT[p]], (r, ring(NZ + p - via))
+        )
+
     for turn, (h, p) in enumerate((h, p) for h in range(2) for p in LEAF):
         c_copies[h, p].wait_recv()
         c_share(h, p)
-        if turn == 12:
+        if turn == 8:
             wait(erecv.at[pl.ds(1, 2 * NP - 1)], e_rs)
             acc = epart[r, core].astype(F32)
             for n in range(1, 2 * NP):
                 acc = acc + erecv[n].astype(F32)
             zall[z] = acc.astype(BF16)
-            for i in (8, 7, 9, 6, 10, 5, 11, 4, 12, 3, 13, 2, 14, 1, 15):
-                send(zall.at[z], zall.at[z], z_ss.at[0], z_rs.at[0], (r, ring(i)))
+            for p in RELAY + NEAR:
+                z_send(p, 0)
 
     wait(dagg.at[pl.ds(0, NZ)], cs_rs)
 
@@ -254,6 +266,11 @@
             q_copies[i] = send(
                 qpart.at[i], qrecv.at[i], q_ss.at[0], q_rs.at[i], (plane(i), c)
             )
+    for via in RELAY:
+        z_copies[via].wait_recv()
+        for p, relay in LEAF.items():
+            if relay == via:
+                z_send(p, via)
     wait(feats.at[pl.ds(0, NP - 1)], a_ss)
     wait(part, p_ss)
     wait(bsend.at[pl.ds(0, NZ - 1)], b_ss)
@@ -261,7 +278,8 @@
     wait(dagg.at[pl.ds(0, NZ)], cs_ss)
     wait(erecv.at[pl.ds(1, 2 * NP - 1)], e_ss)
 
-    wait(zall.at[pl.ds(0, NZ - 1)], z_rs)
+    for p in NEAR + list(LEAF):
+        z_copies[p].wait_recv()
     acc = zall[0].astype(F32)
     for i in range(1, NZ):
         acc = acc + zall[i].astype(F32)
@@ -333,7 +351,7 @@
             pltpu.VMEM((NZ, 16, T), BF16),
             pltpu.VMEM((NP, 2, 16, T), F32),
         ]
-        + [dma((n,)) for n in (8, 1, 1, 1, 4, 1, 20, 1, 30, 1, 1, 1, 16, 1, 1, 1, 1, 1, 1)],
+        + [dma((n,)) for n in (8, 1, 1, 1, 4, 1, 20, 1, 30, 1, 1, 1, 16, 1, 1, 1, 15, 1, 1)],
         compiler_params=pltpu.CompilerParams(
             collective_id=0, has_side_effects=True, vmem_limit_bytes=60 * 1024 * 1024
         ),

time: 68.7 us -> 67.7 us (0.985)
  Pallas kernels: 67.3 us -> 66.2 us
    pallas_call x1, Pallas kernels: 65.6 us -> 64.6 us  [on_device(): pl.pallas_call(kernel, out_shape=shapes, in_specs=[hbm] * 8, out_specs=(v...]
where the time goes in v6:
time: 67.7 us; the launch traced here: 67.5 us
  Pallas kernels  66.2 us (98%)
  between operations  1.29 us (2%)
    pallas_call x1, Pallas kernels, on_device(): pl.pallas_call(kernel, out_shape=shapes, in_specs=[hbm] * 8, out_specs=(v...  64.6 us
    pallas_call x1, Pallas kernels, on_device(): pl.pallas_call(write_out, out_shape=shapes, in_specs=[vmem] * 4, out_spec...  1.69 us

profile of v6, /device:TPU:1, one launch (start us, length us, event | category | flops | bytes accessed | tf_op | source)
XLA Modules:
  0.0 67.5 jit_solution(2121122423130634056)
XLA Ops:
  1.3 64.6 %shard_map.111 = (bf16[128,256]{1,0:T(8,128)(2,1)}, bf16[128,128]{1,0:T(8,128)(2,1)}, f32[128,256]{1,0:T(8,128)}, f32[1,256]{1,0:T(1,128)}) custom-call(bf16[128,128]{1,0:T(8,128)(2,1)} %feat.1, bf16[16,128,128]{2,1,0:T(8,128)(2,1)} %bitcast.7, s32[16]{0:T(128)} %bitcast.9, s32[16]{0:T(128)} %bitcast.10, s32[1]{0:T(128)} %bitcast.6.count_hbm, ...), custom_call_target="tpu_custom_call" | custom-call | tf_op jit(solution)/shard_map/pallas_call | solution.py:326
  65.8 1.7 %shard_map.112 = (bf16[128,256]{1,0:T(8,128)(2,1)}, bf16[128,128]{1,0:T(8,128)(2,1)}, f32[128,256]{1,0:T(8,128)}, f32[1,256]{1,0:T(1,128)}) custom-call(bf16[128,256]{1,0:T(8,128)(2,1)} %get-tuple-element.12.refs_0_, bf16[128,128]{1,0:T(8,128)(2,1)} %get-tuple-element.13.refs_1_, f32[128,256]{1,0:T(8,128)} %get-tuple-element.14.refs_2_, ...), custom_call_target="tpu_custom_call" | custom-call | tf_op jit(solution)/shard_map/pallas_call | solution.py:368

commit v7 on v6

--- a/solution.py
+++ b/solution.py
@@ -243,7 +243,7 @@
     for turn, (h, p) in enumerate((h, p) for h in range(2) for p in LEAF):
         c_copies[h, p].wait_recv()
         c_share(h, p)
-        if turn == 8:
+        if turn == 5:
             wait(erecv.at[pl.ds(1, 2 * NP - 1)], e_rs)
             acc = epart[r, core].astype(F32)
             for n in range(1, 2 * NP):

time: 67.7 us -> 67.4 us (level)
  no operation moved by 1% of the time
where the time goes in v7:
time: 67.4 us; the launch traced here: 67.2 us
  Pallas kernels  65.9 us (98%)
  between operations  1.29 us (2%)
    pallas_call x1, Pallas kernels, on_device(): pl.pallas_call(kernel, out_shape=shapes, in_specs=[hbm] * 8, out_specs=(v...  64.2 us
    pallas_call x1, Pallas kernels, on_device(): pl.pallas_call(write_out, out_shape=shapes, in_specs=[vmem] * 4, out_spec...  1.69 us

profile of v7, /device:TPU:1, one launch (start us, length us, event | category | flops | bytes accessed | tf_op | source)
XLA Modules:
  0.0 67.2 jit_solution(7405896565052599938)
XLA Ops:
  1.3 64.2 %shard_map.111 = (bf16[128,256]{1,0:T(8,128)(2,1)}, bf16[128,128]{1,0:T(8,128)(2,1)}, f32[128,256]{1,0:T(8,128)}, f32[1,256]{1,0:T(1,128)}) custom-call(bf16[128,128]{1,0:T(8,128)(2,1)} %feat.1, bf16[16,128,128]{2,1,0:T(8,128)(2,1)} %bitcast.7, s32[16]{0:T(128)} %bitcast.9, s32[16]{0:T(128)} %bitcast.10, s32[1]{0:T(128)} %bitcast.6.count_hbm, ...), custom_call_target="tpu_custom_call" | custom-call | tf_op jit(solution)/shard_map/pallas_call | solution.py:326
  65.5 1.7 %shard_map.112 = (bf16[128,256]{1,0:T(8,128)(2,1)}, bf16[128,128]{1,0:T(8,128)(2,1)}, f32[128,256]{1,0:T(8,128)}, f32[1,256]{1,0:T(1,128)}) custom-call(bf16[128,256]{1,0:T(8,128)(2,1)} %get-tuple-element.12.refs_0_, bf16[128,128]{1,0:T(8,128)(2,1)} %get-tuple-element.13.refs_1_, f32[128,256]{1,0:T(8,128)} %get-tuple-element.14.refs_2_, ...), custom_call_target="tpu_custom_call" | custom-call | tf_op jit(solution)/shard_map/pallas_call | solution.py:368
